TPU v7x, 32 devices: a whole 2x2x4 slice. The times are simulated.
32 devices in a mesh: dp: 4 (over y, x), ctx: 8 (over z, core).
Axes of the slice: x: 2, y: 2, z: 4, core: 2. Of those that a mesh axis runs over, the one named last changes fastest.
Arguments:
- queries: bfloat16 [4, 2048, 512], P('dp', 'ctx'), may hold values from -6 to 6
- key_vectors: bfloat16 [4, 2048, 512], P('dp', 'ctx'), may hold values from -6 to 6
- value_vectors: bfloat16 [4, 2048, 512], P('dp', 'ctx'), may hold values from -6 to 6
- grad_output: bfloat16 [4, 2048, 512], P('dp', 'ctx'), may hold values from -768 to 768
- pattern: int32 [4, 16, 2], P('dp', 'ctx'), may hold values from 0 to 1
- lengths: int32 [4, 1], P('dp'), may hold values from 512 to 2048, as said below
- widths: int32 [4, 1], P('dp'), may hold values from 1 to 2, as said below
- relative_bucket_bias: float32 [4, 7], replicated, may hold values from -4 to 4
Outputs:
- grad_queries: bfloat16 [4, 2048, 512], P('dp', 'ctx')
- grad_keys: bfloat16 [4, 2048, 512], P('dp', 'ctx')
- value_row_gradients: bfloat16 [4, 2048, 512], P('dp', 'ctx')
- grad_bias: float32 [4, 7], replicated
Inputs may be any that keep to these rules, and one draw needn't show every extreme that they name: `lengths`: one user has a history of all 2048 events and one has 512. `widths`: some user has the widest band and some the narrowest.
All inputs are finite; a program needn't handle non-finite values.
Results may differ from a plain program's by a relative error of at most 0.005.
Values may be sent and summed in bfloat16 or wider, within the bound.
A program may use at most 64 MiB of HBM per device.

v0:
```python
import jax
import jax.numpy as jnp
from jax import lax
from jax.sharding import PartitionSpec as P

BLOCK = 128
GROUP = 8
FAR = 2
NBUCK = 7
SEQ = 2048


def from_behind(array, axis, by):
    size = lax.axis_size(axis)
    pairs = [(i, i + by) for i in range(size) if 0 <= i + by < size]
    return lax.ppermute(array, axis, pairs)


def tile_grads(q_rows, g_rows, k_rows, v_rows, keep_mask, buckets, relative_bucket_bias):
    groups, query_len, model_width = q_rows.shape
    key_len = k_rows.shape[1]
    head_count = relative_bucket_bias.shape[0]
    head_dim = model_width // head_count
    q_blocks = query_len // BLOCK
    k_blocks = key_len // BLOCK
    scaling = head_dim ** (-0.5)
    q_heads = q_rows.reshape(groups, query_len, head_count, head_dim)
    g_heads = g_rows.reshape(groups, query_len, head_count, head_dim)
    k_heads = k_rows.reshape(groups, key_len, head_count, head_dim)
    v_heads = v_rows.reshape(groups, key_len, head_count, head_dim)
    onehot = (buckets[..., None] == jnp.arange(NBUCK, dtype=jnp.int32)).astype(jnp.float32)
    bias_tile = jnp.einsum(
        "gxyu,hu->ghxy", onehot, relative_bucket_bias, precision=lax.Precision.HIGHEST
    )
    raw_score = jnp.einsum("gqhd,gkhd->ghqk", q_heads, k_heads, preferred_element_type=jnp.float32)
    score = (raw_score * scaling).reshape(groups, head_count, q_blocks, BLOCK, k_blocks, BLOCK)
    score = (score + bias_tile[:, :, :, None, :, None]).reshape(
        groups, head_count, query_len, key_len
    )
    keep = keep_mask[:, None, :, :]
    sigmoid_s = jax.nn.sigmoid(score)
    weights_bf = jnp.where(keep, score * sigmoid_s / SEQ, 0.0).astype(jnp.bfloat16)
    value_gradient = jnp.einsum(
        "ghqk,gqhd->gkhd", weights_bf, g_heads, preferred_element_type=jnp.float32
    )
    grad_prob = jnp.einsum("gqhd,gkhd->ghqk", g_heads, v_heads, preferred_element_type=jnp.float32)
    dscore = jnp.where(keep, grad_prob * (sigmoid_s * (1.0 + score * (1.0 - sigmoid_s))) / SEQ, 0.0)
    dscore_bf = dscore.astype(jnp.bfloat16)
    block_sums = dscore.reshape(groups, head_count, q_blocks, BLOCK, k_blocks, BLOCK).sum(
        axis=(3, 5)
    )
    grad_bias = jnp.einsum("ghxy,gxyu->hu", block_sums, onehot, precision=lax.Precision.HIGHEST)
    grad_q = (
        jnp.einsum("ghqk,gkhd->gqhd", dscore_bf, k_heads, preferred_element_type=jnp.float32)
        * scaling
    )
    key_gradient = (
        jnp.einsum("ghqk,gqhd->gkhd", dscore_bf, q_heads, preferred_element_type=jnp.float32)
        * scaling
    )
    return (
        grad_q.reshape(groups, query_len, model_width),
        key_gradient.reshape(groups, key_len, model_width),
        value_gradient.reshape(groups, key_len, model_width),
        grad_bias,
    )


def local_mask(span_id, length, band_width, token_count):
    blocks = token_count // BLOCK
    places = span_id * token_count + jnp.arange(token_count, dtype=jnp.int32)
    block_ids = jnp.arange(token_count, dtype=jnp.int32) // BLOCK
    allowed = (block_ids[:, None] - block_ids[None, :] <= band_width) & (
        places[None, :] <= places[:, None]
    )
    allowed = allowed & (places[:, None] < length) & (places[None, :] < length)
    grid = jnp.arange(blocks, dtype=jnp.int32)
    buckets = jnp.clip(grid[:, None] - grid[None, :], 0, NBUCK - 1)
    return (allowed[None], buckets[None])


def near_mask(span_id, length, band_width, token_count):
    blocks = token_count // BLOCK
    q_places = span_id * token_count + jnp.arange(token_count, dtype=jnp.int32)
    k_places = (span_id - 1) * token_count + jnp.arange(token_count, dtype=jnp.int32)
    block_ids = jnp.arange(token_count, dtype=jnp.int32) // BLOCK
    distance = block_ids[:, None] + blocks - block_ids[None, :]
    allowed = (distance <= band_width) & (q_places[:, None] < length) & (k_places[None, :] < length)
    allowed = allowed & (span_id >= 1) & (span_id < GROUP)
    grid = jnp.arange(blocks, dtype=jnp.int32)
    buckets = jnp.clip(grid[:, None] + blocks - grid[None, :], 0, NBUCK - 1)
    return (allowed[None], buckets[None])


def far_mask(span_id, chosen, distance, length, token_count):
    blocks = token_count // BLOCK
    grid = jnp.arange(blocks, dtype=jnp.int32)
    inner = jnp.arange(BLOCK, dtype=jnp.int32)
    q_places = span_id * token_count + grid[:, None] * BLOCK + inner[None, :]
    k_places = (span_id - distance) * token_count + chosen[:, None] * BLOCK + inner[None, :]
    allowed = (q_places[:, :, None] < length) & (k_places[:, None, :] < length)
    allowed = allowed & (span_id >= distance) & (span_id < GROUP)
    buckets = jnp.clip(distance * blocks + grid - chosen, 0, NBUCK - 1)[:, None, None]
    return (allowed, buckets)


def local_terms(q_rows, g_rows, k_rows, v_rows, span_id, length, band_width, relative_bucket_bias):
    keep_mask, buckets = local_mask(span_id, length, band_width, q_rows.shape[0])
    grads = tile_grads(
        q_rows[None],
        g_rows[None],
        k_rows[None],
        v_rows[None],
        keep_mask,
        buckets,
        relative_bucket_bias,
    )
    return (grads[0][0], grads[1][0], grads[2][0], grads[3])


def near_terms(q_rows, g_rows, k_rows, v_rows, span_id, length, band_width, relative_bucket_bias):
    keep_mask, buckets = near_mask(span_id, length, band_width, q_rows.shape[0])
    grads = tile_grads(
        q_rows[None],
        g_rows[None],
        k_rows[None],
        v_rows[None],
        keep_mask,
        buckets,
        relative_bucket_bias,
    )
    return (grads[0][0], grads[1][0], grads[2][0], grads[3])


def far_terms(
    q_rows, g_rows, k_rows, v_rows, chosen, span_id, distance, length, relative_bucket_bias
):
    token_count, model_width = q_rows.shape
    blocks = token_count // BLOCK
    keep_mask, buckets = far_mask(span_id, chosen, distance, length, token_count)
    q_tiles = q_rows.reshape(blocks, BLOCK, model_width)
    g_tiles = g_rows.reshape(blocks, BLOCK, model_width)
    k_tiles = jnp.take(k_rows.reshape(blocks, BLOCK, model_width), chosen, axis=0)
    v_tiles = jnp.take(v_rows.reshape(blocks, BLOCK, model_width), chosen, axis=0)
    grad_q, key_gradient, value_gradient, grad_bias = tile_grads(
        q_tiles, g_tiles, k_tiles, v_tiles, keep_mask, buckets, relative_bucket_bias
    )
    selector_matrix = (chosen[:, None] == jnp.arange(blocks, dtype=jnp.int32)[None, :]).astype(
        jnp.float32
    )
    key_gradient = jnp.einsum(
        "as,apc->spc", selector_matrix, key_gradient, precision=lax.Precision.HIGHEST
    ).reshape(token_count, model_width)
    value_gradient = jnp.einsum(
        "as,apc->spc", selector_matrix, value_gradient, precision=lax.Precision.HIGHEST
    ).reshape(token_count, model_width)
    return (grad_q.reshape(token_count, model_width), key_gradient, value_gradient, grad_bias)


def on_device(
    queries, key_vectors, value_vectors, grad_output, pattern, lengths, widths, relative_bucket_bias
):
    position = lax.axis_index("ctx")
    span_id = position % GROUP
    user_slot = position // GROUP
    length = lengths[0, user_slot]
    band_width = widths[0, user_slot]
    q_rows = queries[0]
    k_rows = key_vectors[0]
    v_rows = value_vectors[0]
    g_rows = grad_output[0]
    block_table = pattern[0]
    grad_q, key_gradient, value_gradient, grad_bias = local_terms(
        q_rows, g_rows, k_rows, v_rows, span_id, length, band_width, relative_bucket_bias
    )
    distances = [2**section for section in range(FAR + 1)]
    table_bf = block_table.astype(jnp.bfloat16)
    for section, distance in enumerate(distances):
        far_q, far_g, far_table = from_behind((q_rows, g_rows, table_bf), "ctx", -distance)
        query_span = span_id + distance
        if section == 0:
            terms = near_terms(
                far_q, far_g, k_rows, v_rows, query_span, length, band_width, relative_bucket_bias
            )
        else:
            chosen = far_table[:, section - 1].astype(jnp.int32)
            terms = far_terms(
                far_q,
                far_g,
                k_rows,
                v_rows,
                chosen,
                query_span,
                distance,
                length,
                relative_bucket_bias,
            )
        key_gradient = key_gradient + terms[1]
        value_gradient = value_gradient + terms[2]
        grad_bias = grad_bias + terms[3]
        back_q = from_behind(terms[0], "ctx", distance)
        grad_q = grad_q + back_q
    grad_bias = lax.psum(grad_bias, ("dp", "ctx"))
    return (
        grad_q[None].astype(jnp.bfloat16),
        key_gradient[None].astype(jnp.bfloat16),
        value_gradient[None].astype(jnp.bfloat16),
        grad_bias,
    )


def solution(mesh):
    in_specs = (
        P("dp", "ctx", None),
        P("dp", "ctx", None),
        P("dp", "ctx", None),
        P("dp", "ctx", None),
        P("dp", "ctx", None),
        P("dp", None),
        P("dp", None),
        P(),
    )
    out_specs = (P("dp", "ctx", None), P("dp", "ctx", None), P("dp", "ctx", None), P())
    return jax.shard_map(
        on_device, mesh=mesh, in_specs=in_specs, out_specs=out_specs, check_vma=False
    )
```

profile of v0, /device:TPU:12, one launch (start us, length us, event | category | flops | bytes accessed | tf_op | source)
XLA Modules:
  0.0 182.2 jit_solution(13746353603222092864)
XLA Ops:
  2.8 2.4 %collective-permute-start.3 = (bf16[2,2]{1,0:T(2,128)(2,1)S(1)}, bf16[2,2]{1,0:T(2,128)(2,1)S(1)}, u32[]{:S(2)}, u32[]{:S(2)}) collective-permute-start(bf16[2,2]{1,0:T(2,128)(2,1)S(1)} %convert_bitcast_fusion), channel_id=1, source_target_pairs={{2,0},{3,1},{4,2},{5,3},{6,4},{7,5},{10,8},{11,9},{12,10},{13,11},... | collective-permute-start | bytes 32 | tf_op jit(solution)/shard_map/ppermute | solution.py:16
  8.2 1.9 %collective-permute-start.4 = (bf16[256,512]{0,1:T(8,128)(2,1)}, bf16[256,512]{0,1:T(8,128)(2,1)}, u32[]{:S(2)}, u32[]{:S(2)}) collective-permute-start(bf16[256,512]{0,1:T(8,128)(2,1)} %bitcast.8), channel_id=1, source_target_pairs={{2,0},{3,1},{4,2},{5,3},{6,4},{7,5},{10,8},{11,9},{12,10},{13,11},... | collective-permute-start | bytes 786440 | tf_op jit(solution)/shard_map/ppermute | solution.py:16
  10.1 1.9 %collective-permute-start = (bf16[256,512]{0,1:T(8,128)(2,1)}, bf16[256,512]{0,1:T(8,128)(2,1)}, u32[]{:S(2)}, u32[]{:S(2)}) collective-permute-start(bf16[256,512]{0,1:T(8,128)(2,1)} %bitcast.8), channel_id=1, source_target_pairs={{1,0},{2,1},{3,2},{4,3},{5,4},{6,5},{7,6},{9,8},{10,9},{11,10},{12... | collective-permute-start | bytes 786440 | tf_op jit(solution)/shard_map/ppermute | solution.py:16
  18.4 2.3 %fusion.27 = f32[4,256,128]{1,2,0:T(8,128)} fusion(bf16[256,4,128]{0,2,1:T(8,128)(2,1)} %bitcast.83, f32[4,256,256]{2,1,0:T(8,128)S(1)} %fusion.3, pred[256,256]{1,0:T(8,128)(4,1)S(1)} %get-tuple-element.10), kind=kOutput, calls=%fused_computation.68 | convolution fusion | flops 68943872 | bytes 1900544 | tf_op jit(solution)/shard_map/ghqk,gqhd->gkhd/dot_general | solution.py:43
  26.1 2.1 %add.436 = f32[4,256,256]{2,1,0:T(8,128)S(1)} reshape(f32[4,2,128,2,128]{4,3,2,1,0:T(2,128)} %add.435) | data formatting | bytes 2097152 | tf_op jit(solution)/shard_map/add | solution.py:37
  28.2 2.1 %convolution_multiply_fusion.11 = f32[4,256,128]{1,2,0:T(8,128)} fusion(bf16[256,4,128]{0,2,1:T(8,128)(2,1)} %copy.171, f32[4,256,256]{2,1,0:T(8,128)S(1)} %fusion.5), kind=kOutput, calls=%fused_computation.40 | convolution fusion | flops 67502080 | bytes 1835008 | tf_op jit(solution)/shard_map/ghqk,gkhd->gqhd/dot_general | solution.py:54
  30.3 2.0 %copy.181 = f32[256,512]{1,0:T(8,128)} copy(f32[256,512]{0,1:T(8,128)} %bitcast.209) | data formatting | bytes 1048576 | tf_op jit(solution)/shard_map/squeeze;reshape | solution.py:118
  34.8 1.9 %collective-permute-start.5 = (bf16[256,512]{0,1:T(8,128)(2,1)S(1)}, bf16[256,512]{0,1:T(8,128)(2,1)}, u32[]{:S(2)}, u32[]{:S(2)}) collective-permute-start(bf16[256,512]{0,1:T(8,128)(2,1)S(1)} %bitcast.194), channel_id=1, source_target_pairs={{2,0},{3,1},{4,2},{5,3},{6,4},{7,5},{10,8},{11,9},{12,10},{13,11},... | collective-permute-start | bytes 786440 | tf_op jit(solution)/shard_map/ppermute | solution.py:16
  43.8 11.9 %collective-permute-done.5 = bf16[256,512]{0,1:T(8,128)(2,1)} collective-permute-done((bf16[256,512]{0,1:T(8,128)(2,1)S(1)}, bf16[256,512]{0,1:T(8,128)(2,1)}, u32[]{:S(2)}, u32[]{:S(2)}) %collective-permute-start.5) | collective-permute-done | bytes 262176 | tf_op jit(solution)/shard_map/ppermute | solution.py:16
  55.7 2.1 %collective-permute-start.1 = (bf16[256,512]{0,1:T(8,128)(2,1)S(1)}, bf16[256,512]{0,1:T(8,128)(2,1)S(1)}, u32[]{:S(2)}, u32[]{:S(2)}) collective-permute-start(bf16[256,512]{0,1:T(8,128)(2,1)S(1)} %bitcast.195), channel_id=1, source_target_pairs={{1,0},{2,1},{3,2},{4,3},{5,4},{6,5},{7,6},{9,8},{10,9},{11,10},{12... | collective-permute-start | bytes 786440 | tf_op jit(solution)/shard_map/ppermute | solution.py:16
  61.4 2.1 %fusion.107 = (f32[2,4]{1,0:T(2,128)}, bf16[2,4,128,128]{2,3,1,0:T(8,128)(2,1)S(1)}) fusion(f32[2,4,128,128]{2,3,1,0:T(8,128)S(1)} %fusion.19, bf16[2,128,4,128]{1,3,2,0:T(8,128)(2,1)} %bitcast.221, bf16[2,128,4,128]{1,0,3,2:T(2,128)(2,1)} %reshape.840, pred[2,128,128]{1,2,0:T(8,128)(4,1)S(1)} %and_and_fusion.1), kind=kOutput, calls=%fused_computation.191 | convolution fusion | flops 35127288 | bytes 1343520 | tf_op jit(solution)/shard_map/gqhd,gkhd->ghqk/dot_general | solution.py:46
  70.3 2.2 %fusion.108 = (f32[2,4]{1,0:T(2,128)}, bf16[2,4,128,128]{2,3,1,0:T(8,128)(2,1)S(1)}) fusion(f32[2,4,128,128]{2,3,1,0:T(8,128)} %fusion.16, bf16[2,128,4,128]{1,3,2,0:T(8,128)(2,1)S(1)} %bitcast.220, bf16[2,128,4,128]{1,0,3,2:T(2,128)(2,1)} %reshape.842, pred[2,128,128]{1,2,0:T(8,128)(4,1)S(1)} %and_and_fusion), kind=kOutput, calls=%fused_computation.192 | convolution fusion | flops 35127288 | bytes 1343520 | tf_op jit(solution)/shard_map/gqhd,gkhd->ghqk/dot_general | solution.py:46
  82.8 2.0 %copy.191 = f32[2,128,4,128]{3,2,1,0:T(4,128)} copy(f32[2,128,4,128]{1,3,2,0:T(8,128)} %fusion.17) | data formatting | bytes 1048576 | tf_op jit(solution)/shard_map/mul | solution.py:54
  86.7 2.0 %copy.206 = f32[2,128,4,128]{1,3,2,0:T(8,128)} copy(f32[2,128,4,128]{3,1,2,0:T(8,128)} %fusion.13) | data formatting | bytes 1048576 | tf_op jit(solution)/shard_map/mul | solution.py:58
  88.8 2.0 %copy.207 = f32[2,128,512]{2,0,1:T(2,128)} copy(f32[2,128,512]{1,2,0:T(8,128)} %bitcast.211) | data formatting | bytes 1048576 | tf_op jit(solution)/shard_map/reshape | solution.py:63
  90.8 2.1 %fusion.73 = f32[2,128,512]{2,0,1:T(2,128)S(1)} fusion(f32[2,128,512]{2,0,1:T(2,128)} %copy.207, s32[2]{0:T(128)S(1)} %get-tuple-element.6), kind=kOutput, calls=%fused_computation.131 | convolution fusion | flops 3145732 | bytes 1048584 | tf_op jit(solution)/shard_map/as,apc->spc/dot_general | solution.py:151
  93.8 2.0 %copy.224 = f32[2,128,512]{2,0,1:T(2,128)} copy(f32[2,128,512]{1,2,0:T(8,128)} %bitcast.217) | data formatting | bytes 1048576 | tf_op jit(solution)/shard_map/reshape | solution.py:64
  95.9 2.1 %fusion.67 = f32[2,128,512]{2,0,1:T(2,128)S(1)} fusion(f32[2,128,512]{2,0,1:T(2,128)} %copy.224, s32[2]{0:T(128)S(1)} %get-tuple-element.8), kind=kOutput, calls=%fused_computation.125 | convolution fusion | flops 3145732 | bytes 1048584 | tf_op jit(solution)/shard_map/as,apc->spc/dot_general | solution.py:154
  98.9 2.0 %copy.201 = f32[2,128,4,128]{3,2,1,0:T(4,128)} copy(f32[2,128,4,128]{1,3,2,0:T(8,128)} %fusion.14) | data formatting | bytes 1048576 | tf_op jit(solution)/shard_map/mul | solution.py:54
  100.9 1.9 %copy.292 = f32[32,8,4,128]{3,1,2,0:T(8,128)} copy(f32[32,8,4,128]{3,2,1,0:T(4,128)} %bitcast.212) | data formatting | bytes 1048576
  102.8 2.0 %copy.213 = f32[2,128,4,128]{1,3,2,0:T(8,128)} copy(f32[2,128,4,128]{3,1,2,0:T(8,128)} %fusion.12) | data formatting | bytes 1048576 | tf_op jit(solution)/shard_map/mul | solution.py:58
  104.8 2.0 %copy.214 = f32[2,128,512]{2,0,1:T(2,128)} copy(f32[2,128,512]{1,2,0:T(8,128)} %bitcast.213) | data formatting | bytes 1048576 | tf_op jit(solution)/shard_map/reshape | solution.py:63
  106.9 2.2 %fusion.69 = f32[2,128,512]{2,0,1:T(2,128)S(1)} fusion(f32[2,128,512]{2,0,1:T(2,128)} %copy.214, s32[2]{0:T(128)S(1)} %get-tuple-element.8), kind=kOutput, calls=%fused_computation.127 | convolution fusion | flops 3145732 | bytes 1048584 | tf_op jit(solution)/shard_map/as,apc->spc/dot_general | solution.py:151
  110.0 3.1 %collective-permute-start.10 = (f32[256,512]{1,0:T(8,128)}, f32[256,512]{1,0:T(8,128)}, u32[]{:S(2)}, u32[]{:S(2)}) collective-permute-start(f32[256,512]{1,0:T(8,128)} %bitcast.181), channel_id=1, source_target_pairs={{0,4},{1,5},{2,6},{3,7},{8,12},{9,13},{10,14},{11,15},{16,20},{17,... | collective-permute-start | bytes 1572872 | tf_op jit(solution)/shard_map/ppermute | solution.py:16
  113.1 2.1 %collective-permute-start.6 = (f32[256,512]{1,0:T(8,128)}, f32[256,512]{1,0:T(8,128)}, u32[]{:S(2)}, u32[]{:S(2)}) collective-permute-start(f32[256,512]{1,0:T(8,128)} %bitcast.182), channel_id=1, source_target_pairs={{0,2},{1,3},{2,4},{3,5},{4,6},{5,7},{8,10},{9,11},{10,12},{11,13},... | collective-permute-start | bytes 1572872 | tf_op jit(solution)/shard_map/ppermute | solution.py:16
  115.2 2.2 %convolution_add_fusion = f32[4,256,128]{1,2,0:T(8,128)} fusion(f32[4,256,128]{1,2,0:T(8,128)S(1)} %copy-done.35, bf16[256,4,128]{0,2,1:T(8,128)(2,1)} %bitcast.9, f32[4,256,256]{2,1,0:T(8,128)S(1)} %copy-done.15, pred[256,256]{1,0:T(8,128)(4,1)S(1)} %get-tuple-element.9), kind=kOutput, calls=%fused_computation.36 | convolution fusion | flops 69074944 | bytes 2424832 | tf_op jit(solution)/shard_map/ghqk,gqhd->gkhd/dot_general | solution.py:43
  117.4 2.0 %copy.221 = f32[1,256,512]{2,1,0:T(8,128)} copy(f32[1,256,512]{1,2,0:T(8,128)} %bitcast.219) | data formatting | bytes 1048576 | tf_op jit(solution)/shard_map/add | solution.py:199
  119.5 2.1 %fusion.20 = f32[4,256,128]{1,2,0:T(8,128)} fusion(f32[4,256,128]{1,2,0:T(8,128)} %fusion.33, bf16[256,4,128]{0,2,1:T(8,128)(2,1)S(1)} %bitcast.216, f32[4,256,256]{2,1,0:T(8,128)S(1)} %fusion.2), kind=kOutput, calls=%fused_computation.38 | convolution fusion | flops 67633152 | bytes 2359296 | tf_op jit(solution)/shard_map/ghqk,gqhd->gkhd/dot_general | solution.py:58
  127.2 42.2 %psum.7 = f32[4,7]{1,0:T(4,128)} all-reduce(f32[4,7]{1,0:T(4,128)S(1)} %convolution_add_fusion.2), channel_id=1, replica_groups=mesh['dp'=4,'ctx'=8] {'dp','ctx'}, use_global_device_ids=true, to_apply=%region_4.6 | all-reduce | flops 28 | bytes 224 | tf_op jit(solution)/shard_map/psum | solution.py:203
  169.4 1.9 %collective-permute-start.2 = (f32[256,512]{1,0:T(8,128)}, f32[256,512]{1,0:T(8,128)S(1)}, u32[]{:S(2)}, u32[]{:S(2)}) collective-permute-start(f32[256,512]{1,0:T(8,128)} %copy.180), channel_id=1, source_target_pairs={{0,1},{1,2},{2,3},{3,4},{4,5},{5,6},{6,7},{8,9},{9,10},{10,11},{11... | collective-permute-start | bytes 1572872 | tf_op jit(solution)/shard_map/ppermute | solution.py:16
  173.5 6.6 %collective-permute-done.2 = f32[256,512]{1,0:T(8,128)S(1)} collective-permute-done((f32[256,512]{1,0:T(8,128)}, f32[256,512]{1,0:T(8,128)S(1)}, u32[]{:S(2)}, u32[]{:S(2)}) %collective-permute-start.2) | collective-permute-done | bytes 524320 | tf_op jit(solution)/shard_map/ppermute | solution.py:16
  180.1 2.1 %fusion.30 = bf16[1,256,512]{2,1,0:T(8,128)(2,1)} fusion(f32[256,512]{1,0:T(8,128)} %collective-permute-done.10, f32[256,512]{1,0:T(8,128)} %collective-permute-done.6, f32[256,512]{1,0:T(8,128)S(1)} %copy-done.13, f32[256,512]{1,0:T(8,128)S(1)} %collective-permute-done.2), kind=kLoop, calls=%fused_computation.71 | loop fusion | flops 524288 | bytes 2359296 | tf_op jit(solution)/shard_map/convert_element_type | solution.py:205
  (167 shorter events, 57.8 us)
Async XLA Ops:
  0.6 12.8 %copy-start = (f32[4,7]{1,0:T(4,128)S(1)}, f32[4,7]{1,0:T(4,128)}, u32[]{:S(2)}) copy-start(f32[4,7]{1,0:T(4,128)} %param.17) | copy-start | bytes 340
  1.3 12.4 %copy-start.7 = (bf16[1,256,512]{2,1,0:T(8,128)(2,1)S(1)}, bf16[1,256,512]{2,1,0:T(8,128)(2,1)}, u32[]{:S(2)}) copy-start(bf16[1,256,512]{2,1,0:T(8,128)(2,1)} %param.11) | copy-start | bytes 786436
  1.3 31.4 %collective-permute-start.7 = (bf16[2,2]{1,0:T(2,128)(2,1)S(1)}, bf16[2,2]{1,0:T(2,128)(2,1)S(1)}, u32[]{:S(2)}, u32[]{:S(2)}) collective-permute-start(bf16[2,2]{1,0:T(2,128)(2,1)S(1)} %convert_bitcast_fusion), channel_id=1, source_target_pairs={{4,0},{5,1},{6,2},{7,3},{12,8},{13,9},{14,10},{15,11},{20,16},{21,... | collective-permute-start | bytes 32 | tf_op jit(solution)/shard_map/ppermute | solution.py:16
  2.8 32.0 %collective-permute-start.3 = (bf16[2,2]{1,0:T(2,128)(2,1)S(1)}, bf16[2,2]{1,0:T(2,128)(2,1)S(1)}, u32[]{:S(2)}, u32[]{:S(2)}) collective-permute-start(bf16[2,2]{1,0:T(2,128)(2,1)S(1)} %convert_bitcast_fusion), channel_id=1, source_target_pairs={{2,0},{3,1},{4,2},{5,3},{6,4},{7,5},{10,8},{11,9},{12,10},{13,11},... | collective-permute-start | bytes 32 | tf_op jit(solution)/shard_map/ppermute | solution.py:16
  6.9 61.6 %collective-permute-start.8 = (bf16[256,512]{0,1:T(8,128)(2,1)}, bf16[256,512]{0,1:T(8,128)(2,1)}, u32[]{:S(2)}, u32[]{:S(2)}) collective-permute-start(bf16[256,512]{0,1:T(8,128)(2,1)} %bitcast.8), channel_id=1, source_target_pairs={{4,0},{5,1},{6,2},{7,3},{12,8},{13,9},{14,10},{15,11},{20,16},{21,... | collective-permute-start | bytes 786440 | tf_op jit(solution)/shard_map/ppermute | solution.py:16
  8.2 51.5 %collective-permute-start.4 = (bf16[256,512]{0,1:T(8,128)(2,1)}, bf16[256,512]{0,1:T(8,128)(2,1)}, u32[]{:S(2)}, u32[]{:S(2)}) collective-permute-start(bf16[256,512]{0,1:T(8,128)(2,1)} %bitcast.8), channel_id=1, source_target_pairs={{2,0},{3,1},{4,2},{5,3},{6,4},{7,5},{10,8},{11,9},{12,10},{13,11},... | collective-permute-start | bytes 786440 | tf_op jit(solution)/shard_map/ppermute | solution.py:16
  10.1 67.7 %collective-permute-start = (bf16[256,512]{0,1:T(8,128)(2,1)}, bf16[256,512]{0,1:T(8,128)(2,1)}, u32[]{:S(2)}, u32[]{:S(2)}) collective-permute-start(bf16[256,512]{0,1:T(8,128)(2,1)} %bitcast.8), channel_id=1, source_target_pairs={{1,0},{2,1},{3,2},{4,3},{5,4},{6,5},{7,6},{9,8},{10,9},{11,10},{12... | collective-permute-start | bytes 786440 | tf_op jit(solution)/shard_map/ppermute | solution.py:16
  12.1 1.3 copy-start.31
  15.7 2.0 %copy-start.2 = (bf16[1,256,512]{1,2,0:T(8,128)(2,1)}, bf16[1,256,512]{1,2,0:T(8,128)(2,1)S(1)}, u32[]{:S(2)}) copy-start(bf16[1,256,512]{1,2,0:T(8,128)(2,1)S(1)} %copy.255) | copy-start | bytes 786436
  18.4 2.3 %copy-start.18 = (bf16[256,4,128]{2,1,0:T(4,128)(2,1)S(1)}, bf16[256,4,128]{2,1,0:T(4,128)(2,1)}, u32[]{:S(2)}) copy-start(bf16[256,4,128]{2,1,0:T(4,128)(2,1)} %reshape.770) | copy-start | bytes 786436
  20.6 1.6 copy-start.3
  32.3 4.6 %copy-start.6 = (bf16[1,256,512]{2,1,0:T(8,128)(2,1)S(1)}, bf16[1,256,512]{2,1,0:T(8,128)(2,1)}, u32[]{:S(2)}) copy-start(bf16[1,256,512]{2,1,0:T(8,128)(2,1)} %param.12) | copy-start | bytes 786436
  33.3 32.4 %collective-permute-start.9 = (bf16[256,512]{0,1:T(8,128)(2,1)S(1)}, bf16[256,512]{0,1:T(8,128)(2,1)}, u32[]{:S(2)}, u32[]{:S(2)}) collective-permute-start(bf16[256,512]{0,1:T(8,128)(2,1)S(1)} %bitcast.193), channel_id=1, source_target_pairs={{4,0},{5,1},{6,2},{7,3},{12,8},{13,9},{14,10},{15,11},{20,16},{21,... | collective-permute-start | bytes 786440 | tf_op jit(solution)/shard_map/ppermute | solution.py:16
  34.8 5.5 %copy-start.27 = (s32[2]{0:T(128)}, s32[2]{0:T(128)S(1)}, u32[]{:S(2)}) copy-start(s32[2]{0:T(128)S(1)} %get-tuple-element.15) | copy-start | bytes 28
  34.8 20.9 %collective-permute-start.5 = (bf16[256,512]{0,1:T(8,128)(2,1)S(1)}, bf16[256,512]{0,1:T(8,128)(2,1)}, u32[]{:S(2)}, u32[]{:S(2)}) collective-permute-start(bf16[256,512]{0,1:T(8,128)(2,1)S(1)} %bitcast.194), channel_id=1, source_target_pairs={{2,0},{3,1},{4,2},{5,3},{6,4},{7,5},{10,8},{11,9},{12,10},{13,11},... | collective-permute-start | bytes 786440 | tf_op jit(solution)/shard_map/ppermute | solution.py:16
  36.9 4.1 %copy-start.29 = (s32[2]{0:T(128)}, s32[2]{0:T(128)S(1)}, u32[]{:S(2)}) copy-start(s32[2]{0:T(128)S(1)} %get-tuple-element.11) | copy-start | bytes 28
  55.7 19.0 %collective-permute-start.1 = (bf16[256,512]{0,1:T(8,128)(2,1)S(1)}, bf16[256,512]{0,1:T(8,128)(2,1)S(1)}, u32[]{:S(2)}, u32[]{:S(2)}) collective-permute-start(bf16[256,512]{0,1:T(8,128)(2,1)S(1)} %bitcast.195), channel_id=1, source_target_pairs={{1,0},{2,1},{3,2},{4,3},{5,4},{6,5},{7,6},{9,8},{10,9},{11,10},{12... | collective-permute-start | bytes 786440 | tf_op jit(solution)/shard_map/ppermute | solution.py:16
  68.5 1.8 copy-start.20
  75.0 2.8 %copy-start.14 = (f32[4,256,256]{2,1,0:T(8,128)}, f32[4,256,256]{2,1,0:T(8,128)S(1)}, u32[]{:S(2)}) copy-start(f32[4,256,256]{2,1,0:T(8,128)S(1)} %fusion) | copy-start | bytes 3145732
  75.0 1.4 copy-start.16
  75.0 1.7 copy-start.22
  76.7 1.2 copy-start.19
  77.9 1.6 copy-start.1
  106.9 8.3 %copy-start.15 = (f32[4,256,256]{2,1,0:T(8,128)S(1)}, f32[4,256,256]{2,1,0:T(8,128)}, u32[]{:S(2)}) copy-start(f32[4,256,256]{2,1,0:T(8,128)} %copy-done.14) | copy-start | bytes 3145732
  109.1 6.2 %copy-start.35 = (f32[4,256,128]{1,2,0:T(8,128)S(1)}, f32[4,256,128]{1,2,0:T(8,128)}, u32[]{:S(2)}) copy-start(f32[4,256,128]{1,2,0:T(8,128)} %fusion.27) | copy-start | bytes 1572868
  110.0 63.5 %collective-permute-start.10 = (f32[256,512]{1,0:T(8,128)}, f32[256,512]{1,0:T(8,128)}, u32[]{:S(2)}, u32[]{:S(2)}) collective-permute-start(f32[256,512]{1,0:T(8,128)} %bitcast.181), channel_id=1, source_target_pairs={{0,4},{1,5},{2,6},{3,7},{8,12},{9,13},{10,14},{11,15},{16,20},{17,... | collective-permute-start | bytes 1572872 | tf_op jit(solution)/shard_map/ppermute | solution.py:16
  113.1 60.4 %collective-permute-start.6 = (f32[256,512]{1,0:T(8,128)}, f32[256,512]{1,0:T(8,128)}, u32[]{:S(2)}, u32[]{:S(2)}) collective-permute-start(f32[256,512]{1,0:T(8,128)} %bitcast.182), channel_id=1, source_target_pairs={{0,2},{1,3},{2,4},{3,5},{4,6},{5,7},{8,10},{9,11},{10,12},{11,13},... | collective-permute-start | bytes 1572872 | tf_op jit(solution)/shard_map/ppermute | solution.py:16
  126.1 45.2 %copy-start.10 = (f32[2,128,512]{2,1,0:T(8,128)S(1)}, f32[2,128,512]{2,1,0:T(8,128)}, u32[]{:S(2)}) copy-start(f32[2,128,512]{2,1,0:T(8,128)} %copy.225) | copy-start | bytes 1572868
  126.1 45.2 %copy-start.12 = (f32[1,256,512]{2,1,0:T(8,128)S(1)}, f32[1,256,512]{2,1,0:T(8,128)}, u32[]{:S(2)}) copy-start(f32[1,256,512]{2,1,0:T(8,128)} %copy.221) | copy-start | bytes 1572868
  169.4 10.7 %collective-permute-start.2 = (f32[256,512]{1,0:T(8,128)}, f32[256,512]{1,0:T(8,128)S(1)}, u32[]{:S(2)}, u32[]{:S(2)}) collective-permute-start(f32[256,512]{1,0:T(8,128)} %copy.180), channel_id=1, source_target_pairs={{0,1},{1,2},{2,3},{3,4},{4,5},{5,6},{6,7},{8,9},{9,10},{10,11},{11... | collective-permute-start | bytes 1572872 | tf_op jit(solution)/shard_map/ppermute | solution.py:16
  171.3 1.3 copy-start.11
  172.6 7.5 %copy-start.13 = (f32[256,512]{1,0:T(8,128)S(1)}, f32[256,512]{1,0:T(8,128)}, u32[]{:S(2)}) copy-start(f32[256,512]{1,0:T(8,128)} %copy.181) | copy-start | bytes 1572868
  (15 other events, 12.0 us)
where the time goes:
time: 184 us; the launch traced here: 182 us
  local copies, waits for them, and re-layouts  54.7 us (30%)
  blocking collectives  42.2 us (23%)
  matrix products  36.1 us (20%)
  starting transfers between devices  21.3 us (12%)
  waiting for transfers between devices  18.6 us (10%)
  other arithmetic  6.7 us (4%)
  between operations  2.64 us (1%)
    psum x1, blocking collectives, on_device(): grad_bias = lax.psum(grad_bias, ('dp', 'ctx'))  42.2 us
    ppermute x11, starting transfers between devices, from_behind(): return lax.ppermute(array, axis, pairs)  21.3 us
    ppermute x11, waiting for transfers between devices, from_behind(): return lax.ppermute(array, axis, pairs)  18.6 us
    unnamed x74, local copies, waits for them, and re-layouts  10.7 us
    dot_general x4, matrix products, tile_grads(): jnp.einsum('gqhd,gkhd->ghqk', g_heads, v_heads, preferred_element_type=jn...  7.51 us
    dot_general x4, matrix products, tile_grads(): jnp.einsum('ghqk,gqhd->gkhd', weights_bf, g_heads, preferred_element_type...  6.73 us
    dot_general x4, matrix products, tile_grads(): jnp.einsum('ghqk,gqhd->gkhd', dscore_bf, q_heads, preferred_element_type=...  5.31 us
    add x4, local copies, waits for them, and re-layouts, tile_grads(): score + bias_tile[:, :, :, None, :, None]  4.55 us
  transfers between devices with their start and end apart: 11, of which 2 were waited for; matrix products, arithmetic and copies ran while one was open for 31% of the time, Pallas kernels for 0%

commit v1 on v0

v1 whole, which is shorter than its diff:
```python
import functools

import jax
import jax.numpy as jnp
from jax import lax
from jax.experimental import pallas as pl
from jax.experimental.pallas import tpu as pltpu
from jax.sharding import PartitionSpec as P

BLOCK = 128
GROUP = 8
NBUCK = 7
SEQ = 2048
F32 = jnp.float32
BF16 = jnp.bfloat16
MESH = pl.DeviceIdType.MESH


def dot(a, b, dims):
    return lax.dot_general(a, b, (dims, ((), ())), preferred_element_type=F32)


def tile(q, g, k, v, bias, scaling, keep=None):
    score = dot(k, q, ((1,), (1,))) * scaling + bias
    gate = jax.nn.sigmoid(score)
    prob = score * gate
    ds = dot(v, g, ((1,), (1,))) * (gate + prob * (1.0 - gate))
    if keep is not None:
        prob = jnp.where(keep, prob, 0.0)
        ds = jnp.where(keep, ds, 0.0)
    prob_bf = prob.astype(BF16)
    ds_bf = ds.astype(BF16)
    grad_v = dot(prob_bf, g, ((1,), (0,)))
    grad_k = dot(ds_bf, q, ((1,), (0,)))
    grad_q = dot(ds_bf, k, ((0,), (0,)))
    return grad_q, grad_k, grad_v, ds


def kernel(
    n_dp, n_ctx, heads, tokens, scaling,
    len_ref, wid_ref, pat_ref, bias_ref, q_ref, k_ref, v_ref, g_ref,
    gq_ref, gk_ref, gv_ref, gb_ref,
    kh, vh, x0, x1, x2, x4, pt0, pt2, pt4, d1, d2, d4, r1, r2, r4, aq, ak, av, ab,
    bt, bc, bd, tsq,
    sa, ra, sb, rb, sc, rc, sp2, rp2, sp4, rp4, sd1, rd1, sd2, rd2, sd4, rd4,
    sbc, rbc, sbd, rbd,
):
    me = lax.axis_index("ctx")
    row = lax.axis_index("dp")
    span = lax.rem(me, GROUP)
    even = lax.rem(me, 2) == 0
    blocks = tokens // BLOCK
    last = GROUP - 1

    def at(shift):
        return (row, me + shift)

    def send(src, dst, s, r, where):
        return pltpu.make_async_remote_copy(
            src_ref=src, dst_ref=dst, send_sem=s, recv_sem=r,
            device_id=where, device_id_type=MESH,
        )

    barrier = pltpu.get_barrier_semaphore()

    @pl.loop(1, n_ctx)
    def _(j):
        pl.semaphore_signal(
            barrier, inc=1, device_id=(row, lax.rem(me + j, n_ctx)), device_id_type=MESH
        )

    @pl.loop(1, n_dp)
    def _(j):
        pl.semaphore_signal(
            barrier, inc=1, device_id=(lax.rem(row + j, n_dp), me), device_id_type=MESH
        )

    slot = me // GROUP
    length = len_ref[0, slot]
    wide = (wid_ref[0, slot] >= 2).astype(F32)
    places = span * tokens + lax.broadcasted_iota(jnp.int32, (tokens, 1), 0)
    real = (places < length).astype(F32)
    real_bf = real.astype(BF16)
    for h in range(heads):
        c = slice(h * BLOCK, (h + 1) * BLOCK)
        x0[h, 0] = q_ref[0, :, c]
        x0[h, 1] = g_ref[0, :, c] * real_bf
    for b in range(blocks):
        for j in range(2):
            pt0[b * 2 + j : b * 2 + j + 1, :] = jnp.full((1, BLOCK), pat_ref[0, b, j].astype(F32))

    pl.semaphore_wait(barrier, n_ctx - 1 + n_dp - 1)

    def copy_a(h):
        return send(x0.at[h], x2.at[h], sa.at[h], ra.at[h], at(-2))

    def copy_b(h):
        return send(x2.at[h], x4.at[h], sb.at[h], rb.at[h], at(-2))

    def copy_c_odd(h):
        return send(x0.at[h], x1.at[h], sc.at[h], rc.at[h], at(-1))

    def copy_c_even(h):
        return send(x2.at[h], x1.at[h], sc.at[h], rc.at[h], at(1))

    def copy_p2():
        return send(pt0, pt2, sp2, rp2, at(-2))

    def copy_p4():
        return send(pt0, pt4, sp4, rp4, at(-4))

    def copy_d(h, d):
        src, dst, s, r = {1: (d1, r1, sd1, rd1), 2: (d2, r2, sd2, rd2), 4: (d4, r4, sd4, rd4)}[d]
        return send(src.at[h], dst.at[h], s.at[h], r.at[h], at(d))

    to2 = span >= 2
    to4 = span >= 4
    from1 = span + 1 <= last
    from2 = span + 2 <= last
    from4 = span + 4 <= last
    relay4 = to2 & from2
    odd_near = jnp.logical_not(even)
    even_near = even & from2

    @pl.when(to2)
    def _():
        copy_p2().start()

        @pl.loop(0, heads)
        def _(h):
            copy_a(h).start()

    @pl.when(to4)
    def _():
        copy_p4().start()

    @pl.when(odd_near)
    def _():
        @pl.loop(0, heads)
        def _(h):
            copy_c_odd(h).start()

    for h in range(heads):
        c = slice(h * BLOCK, (h + 1) * BLOCK)
        kh[h] = k_ref[0, :, c]
        vh[h] = v_ref[0, :, c] * real_bf
    ab[...] = jnp.zeros_like(ab)

    kpos = lax.broadcasted_iota(jnp.int32, (tokens, tokens), 0)
    qpos = lax.broadcasted_iota(jnp.int32, (tokens, tokens), 1)
    kb = kpos // BLOCK
    qb = qpos // BLOCK

    def colsum(x):
        return jnp.sum(x, axis=0, keepdims=True)

    def add_bias(h, bucket, value):
        ab[h, bucket : bucket + 1, :] += value

    @pl.loop(0, heads)
    def _(h):
        bias = jnp.where(qb > kb, bias_ref[h, 1], bias_ref[h, 0])
        gq, gk, gv, ds = tile(
            x0[h, 0], x0[h, 1], kh[h], vh[h], bias, scaling, kpos <= qpos
        )
        aq[h] = gq
        ak[h] = gk
        av[h] = gv
        add_bias(h, 0, colsum(ds[:BLOCK, :BLOCK]) + colsum(ds[BLOCK:, BLOCK:]))
        add_bias(h, 1, colsum(ds[:BLOCK, BLOCK:]))

    out_scale = scaling / SEQ

    def far(h, x, pt, d, level, dst):
        for b in range(blocks):
            rows = slice(b * BLOCK, (b + 1) * BLOCK)
            c1 = pt[b * 2 + level : b * 2 + level + 1, :]
            c0 = 1.0 - c1
            k = (kh[h, :BLOCK, :] * c0 + kh[h, BLOCK:, :] * c1).astype(BF16)
            v = (vh[h, :BLOCK, :] * c0 + vh[h, BLOCK:, :] * c1).astype(BF16)
            u0 = min(blocks * d + b, NBUCK - 1)
            u1 = min(blocks * d + b - 1, NBUCK - 1)
            bias = c0 * bias_ref[h, u0] + c1 * bias_ref[h, u1]
            gq, gk, gv, ds = tile(x[h, 0, rows, :], x[h, 1, rows, :], k, v, bias, scaling)
            dst[h, rows, :] = (gq * out_scale).astype(BF16)
            ak[h, :BLOCK, :] += gk * c0
            ak[h, BLOCK:, :] += gk * c1
            av[h, :BLOCK, :] += gv * c0
            av[h, BLOCK:, :] += gv * c1
            total = colsum(ds)
            if u0 == u1:
                add_bias(h, u0, total)
            else:
                add_bias(h, u0, total * c0)
                add_bias(h, u1, total * c1)

    @pl.when(from2)
    def _():
        copy_p2().wait_recv()

    @pl.loop(0, heads)
    def _(h):
        @pl.when(from2)
        def _():
            copy_a(h).wait_recv()

            @pl.when(to2)
            def _():
                copy_b(h).start()

            @pl.when(even)
            def _():
                copy_c_even(h).start()

            far(h, x2, pt2, 2, 0, d2)
            copy_d(h, 2).start()

        @pl.when(from1)
        def _():
            copy_c_odd(h).wait_recv()
            bias = jnp.where(qb + 1 == kb, bias_ref[h, 1], bias_ref[h, 2])
            weight = jnp.where(qb + 1 == kb, 1.0, jnp.where(qb == kb, wide, 0.0))
            gq, gk, gv, ds = tile(
                x1[h, 0], x1[h, 1], kh[h], vh[h], bias, scaling, weight > 0.0
            )
            d1[h] = (gq * out_scale).astype(BF16)
            copy_d(h, 1).start()
            ak[h] += gk
            av[h] += gv
            add_bias(h, 1, colsum(ds[BLOCK:, :BLOCK]))
            add_bias(h, 2, colsum(ds[:BLOCK, :BLOCK]) + colsum(ds[BLOCK:, BLOCK:]))

    @pl.when(from4)
    def _():
        copy_p4().wait_recv()

        @pl.loop(0, heads)
        def _(h):
            copy_b(h).wait_recv()
            far(h, x4, pt4, 4, 1, d4)
            copy_d(h, 4).start()

    lane = lax.broadcasted_iota(jnp.int32, (8, BLOCK), 1)
    mine = jnp.zeros((8, BLOCK), F32)
    for h in range(heads):
        mine += jnp.where(lane == h, jnp.sum(ab[h], axis=1, keepdims=True), 0.0)
    bt[0] = mine * (1.0 / SEQ)

    def copy_bc(j, source):
        peer = lax.rem(me + j, n_ctx)
        return send(bt.at[0], bc.at[source], sbc.at[j], rbc.at[source], (row, peer))

    def copy_bd(j, source):
        peer = lax.rem(row + j, n_dp)
        return send(bt.at[1], bd.at[source], sbd.at[j], rbd.at[source], (peer, me))

    @pl.loop(1, n_ctx)
    def _(j):
        copy_bc(j, me).start()

    for h in range(heads):
        c = slice(h * BLOCK, (h + 1) * BLOCK)
        gk_ref[0, :, c] = (ak[h] * out_scale).astype(BF16)
        gv_ref[0, :, c] = (av[h] * (real * (1.0 / SEQ))).astype(BF16)

    bc[me] = bt[0]

    @pl.loop(1, n_ctx)
    def _(j):
        copy_bc(j, lax.rem(me + j, n_ctx)).wait_recv()

    bt[1] = jnp.sum(bc[...], axis=0)

    @pl.loop(1, n_dp)
    def _(j):
        copy_bd(j, row).start()

    @pl.loop(0, heads)
    def _(h):
        aq[h] = aq[h] * out_scale

        @pl.when(span >= 1)
        def _():
            copy_d(h, 1).wait_recv()
            aq[h] += r1[h].astype(F32)

        @pl.when(span >= 2)
        def _():
            copy_d(h, 2).wait_recv()
            aq[h] += r2[h].astype(F32)

        @pl.when(span >= 4)
        def _():
            copy_d(h, 4).wait_recv()
            aq[h] += r4[h].astype(F32)

    for h in range(heads):
        gq_ref[0, :, h * BLOCK : (h + 1) * BLOCK] = aq[h].astype(BF16)

    bd[row] = bt[1]

    @pl.loop(1, n_dp)
    def _(j):
        copy_bd(j, lax.rem(row + j, n_dp)).wait_recv()

    tsq[...] = jnp.zeros_like(tsq)
    tsq[:8, :] = jnp.sum(bd[...], axis=0)
    gb_ref[...] = tsq[...].T[:heads, :NBUCK]

    @pl.when(to2)
    def _():
        copy_p2().wait_send()

        @pl.loop(0, heads)
        def _(h):
            copy_a(h).wait_send()

    @pl.when(to4)
    def _():
        copy_p4().wait_send()

    @pl.when(relay4)
    def _():
        @pl.loop(0, heads)
        def _(h):
            copy_b(h).wait_send()

    @pl.when(odd_near | even_near)
    def _():
        @pl.loop(0, heads)
        def _(h):
            copy_c_odd(h).wait_send()

    for d, there in ((1, from1), (2, from2), (4, from4)):
        @pl.when(there)
        def _(d=d):
            @pl.loop(0, heads)
            def _(h):
                copy_d(h, d).wait_send()

    @pl.loop(1, n_ctx)
    def _(j):
        copy_bc(j, me).wait_send()

    @pl.loop(1, n_dp)
    def _(j):
        copy_bd(j, row).wait_send()


def on_device(
    queries, key_vectors, value_vectors, grad_output, pattern, lengths, widths, relative_bucket_bias,
    n_dp, n_ctx,
):
    tokens, width = queries.shape[1:]
    heads = relative_bucket_bias.shape[0]
    dim = width // heads
    vm = pl.BlockSpec(memory_space=pltpu.VMEM)
    sm = pl.BlockSpec(memory_space=pltpu.SMEM)
    dma = pltpu.SemaphoreType.DMA
    x = pltpu.VMEM((heads, 2, tokens, dim), BF16)
    half = pltpu.VMEM((heads, tokens, dim), BF16)
    acc = pltpu.VMEM((heads, tokens, dim), F32)
    pat = pltpu.VMEM((8, BLOCK), F32)
    per_head = dma((heads,))
    rows = jax.ShapeDtypeStruct(queries.shape, BF16)
    return pl.pallas_call(
        functools.partial(kernel, n_dp, n_ctx, heads, tokens, dim ** (-0.5)),
        out_shape=(rows, rows, rows, jax.ShapeDtypeStruct(relative_bucket_bias.shape, F32)),
        in_specs=[sm] * 4 + [vm] * 4,
        out_specs=(vm,) * 4,
        scratch_shapes=[half, half, x, x, x, x, pat, pat, pat]
        + [half] * 6
        + [acc] * 3
        + [
            pltpu.VMEM((heads, 8, BLOCK), F32),
            pltpu.VMEM((2, 8, BLOCK), F32),
            pltpu.VMEM((n_ctx, 8, BLOCK), F32),
            pltpu.VMEM((n_dp, 8, BLOCK), F32),
            pltpu.VMEM((BLOCK, BLOCK), F32),
        ]
        + [per_head] * 6
        + [dma, dma, dma, dma]
        + [per_head] * 6
        + [dma((n_ctx,)), dma((n_ctx,)), dma((n_dp,)), dma((n_dp,))],
        compiler_params=pltpu.CompilerParams(
            collective_id=0, has_side_effects=True, vmem_limit_bytes=40 * 2**20
        ),
    )(lengths, widths, pattern, relative_bucket_bias, queries, key_vectors, value_vectors, grad_output)


def solution(mesh):
    split = P("dp", "ctx", None)
    in_specs = (split,) * 5 + (P("dp", None), P("dp", None), P())
    body = functools.partial(on_device, n_dp=mesh.shape["dp"], n_ctx=mesh.shape["ctx"])
    return jax.shard_map(
        body, mesh=mesh, in_specs=in_specs, out_specs=(split,) * 3 + (P(),), check_vma=False
    )
```

time: 184 us -> 47 us (0.26)
  the two profiles are of different devices: /device:TPU:12 before, /device:TPU:16 now
where the time goes in v1:
time: 47 us; the launch traced here: 46.4 us
  Pallas kernels  37.9 us (81%)
  local copies, waits for them, and re-layouts  6.49 us (14%)
  between operations  2 us (4%)
    pallas_call x1, Pallas kernels, on_device(): pl.pallas_call(functools.partial(kernel, n_dp, n_ctx, heads, tokens, dim...  37.9 us
    unnamed x16, local copies, waits for them, and re-layouts  6.49 us

profile of v1, /device:TPU:16, one launch (start us, length us, event | category | flops | bytes accessed | tf_op | source)
XLA Modules:
  0.0 46.4 jit_solution(3917370034469758490)
XLA Ops:
  0.6 0.0 copy-start.4
  1.3 0.0 copy-start.5
  2.0 0.0 copy-done.4
  2.0 0.0 copy-done.5
  2.0 0.0 copy-start
  2.0 0.9 %copy-done = bf16[1,256,512]{2,1,0:T(8,128)(2,1)S(1)} copy-done((bf16[1,256,512]{2,1,0:T(8,128)(2,1)S(1)}, bf16[1,256,512]{2,1,0:T(8,128)(2,1)}, u32[]{:S(2)}) %copy-start) | copy-done | bytes 262168
  2.9 0.0 copy-start.1
  2.9 0.9 %copy-done.1 = bf16[1,256,512]{2,1,0:T(8,128)(2,1)S(1)} copy-done((bf16[1,256,512]{2,1,0:T(8,128)(2,1)S(1)}, bf16[1,256,512]{2,1,0:T(8,128)(2,1)}, u32[]{:S(2)}) %copy-start.1) | copy-done | bytes 262168
  3.9 0.0 copy-start.2
  3.9 0.9 %copy-done.2 = bf16[1,256,512]{2,1,0:T(8,128)(2,1)S(1)} copy-done((bf16[1,256,512]{2,1,0:T(8,128)(2,1)S(1)}, bf16[1,256,512]{2,1,0:T(8,128)(2,1)}, u32[]{:S(2)}) %copy-start.2) | copy-done | bytes 262168
  4.8 0.0 copy-start.3
  4.8 0.9 %copy-done.3 = bf16[1,256,512]{2,1,0:T(8,128)(2,1)S(1)} copy-done((bf16[1,256,512]{2,1,0:T(8,128)(2,1)S(1)}, bf16[1,256,512]{2,1,0:T(8,128)(2,1)}, u32[]{:S(2)}) %copy-start.3) | copy-done | bytes 262168
  5.8 37.9 %shard_map.111 = (bf16[1,256,512]{2,1,0:T(8,128)(2,1)S(1)}, bf16[1,256,512]{2,1,0:T(8,128)(2,1)S(1)}, bf16[1,256,512]{2,1,0:T(8,128)(2,1)S(1)}, f32[4,7]{1,0:T(4,128)S(1)}) custom-call(s32[1,1]{1,0:T(1,128)S(6)} %copy.16.len_ref, s32[1,1]{1,0:T(1,128)S(6)} %copy.17.wid_ref, s32[1,2,2]{2,1,0:T(2,128)S(1)} %copy-done.5, f32[4,7]{1,0:T(4,128)S(1)} %copy-done.4, ...), custom_call_target="tpu_custom_call" | custom-call | tf_op jit(solution)/shard_map/pallas_call | solution.py:366
  43.7 0.7 %copy.18 = bf16[1,256,512]{2,1,0:T(8,128)(2,1)} copy(bf16[1,256,512]{2,1,0:T(8,128)(2,1)S(1)} %get-tuple-element.8) | data formatting | bytes 524288
  44.4 0.7 %copy.19 = bf16[1,256,512]{2,1,0:T(8,128)(2,1)} copy(bf16[1,256,512]{2,1,0:T(8,128)(2,1)S(1)} %get-tuple-element.9) | data formatting | bytes 524288
  45.1 0.7 %copy.20 = bf16[1,256,512]{2,1,0:T(8,128)(2,1)} copy(bf16[1,256,512]{2,1,0:T(8,128)(2,1)S(1)} %get-tuple-element.10) | data formatting | bytes 524288
  45.8 0.6 %copy.21 = f32[4,7]{1,0:T(4,128)} copy(f32[4,7]{1,0:T(4,128)S(1)} %get-tuple-element.11) | data formatting | bytes 224
Async XLA Ops:
  0.6 1.3 %copy-start.4 = (f32[4,7]{1,0:T(4,128)S(1)}, f32[4,7]{1,0:T(4,128)}, u32[]{:S(2)}) copy-start(f32[4,7]{1,0:T(4,128)} %bias_ref.1) | copy-start | bytes 340
  1.3 0.7 %copy-start.5 = (s32[1,2,2]{2,1,0:T(2,128)S(1)}, s32[1,2,2]{2,1,0:T(2,128)}, u32[]{:S(2)}) copy-start(s32[1,2,2]{2,1,0:T(2,128)} %pat_ref.1) | copy-start | bytes 52
  2.0 1.0 %copy-start = (bf16[1,256,512]{2,1,0:T(8,128)(2,1)S(1)}, bf16[1,256,512]{2,1,0:T(8,128)(2,1)}, u32[]{:S(2)}) copy-start(bf16[1,256,512]{2,1,0:T(8,128)(2,1)} %q_ref.1) | copy-start | bytes 786436
  2.9 0.9 %copy-start.1 = (bf16[1,256,512]{2,1,0:T(8,128)(2,1)S(1)}, bf16[1,256,512]{2,1,0:T(8,128)(2,1)}, u32[]{:S(2)}) copy-start(bf16[1,256,512]{2,1,0:T(8,128)(2,1)} %k_ref.1) | copy-start | bytes 786436
  3.9 0.9 %copy-start.2 = (bf16[1,256,512]{2,1,0:T(8,128)(2,1)S(1)}, bf16[1,256,512]{2,1,0:T(8,128)(2,1)}, u32[]{:S(2)}) copy-start(bf16[1,256,512]{2,1,0:T(8,128)(2,1)} %v_ref.1) | copy-start | bytes 786436
  4.8 0.9 %copy-start.3 = (bf16[1,256,512]{2,1,0:T(8,128)(2,1)S(1)}, bf16[1,256,512]{2,1,0:T(8,128)(2,1)}, u32[]{:S(2)}) copy-start(bf16[1,256,512]{2,1,0:T(8,128)(2,1)} %g_ref.1) | copy-start | bytes 786436

commit v2 on v1

--- a/solution.py
+++ b/solution.py
@@ -13,6 +13,7 @@
 SEQ = 2048
 F32 = jnp.float32
 BF16 = jnp.bfloat16
+VMEM_LIMIT = 63 * 2**20
 MESH = pl.DeviceIdType.MESH
 
 
@@ -38,8 +39,9 @@
 
 def kernel(
     n_dp, n_ctx, heads, tokens, scaling,
-    len_ref, wid_ref, pat_ref, bias_ref, q_ref, k_ref, v_ref, g_ref,
+    len_in, wid_in, pat_in, bias_in, q_ref, k_ref, v_ref, g_ref,
     gq_ref, gk_ref, gv_ref, gb_ref,
+    len_ref, wid_ref, pat_ref, bias_ref, sem_small, sem_q, sem_g, sem_k, sem_v,
     kh, vh, x0, x1, x2, x4, pt0, pt2, pt4, d1, d2, d4, r1, r2, r4, aq, ak, av, ab,
     bt, bc, bd, tsq,
     sa, ra, sb, rb, sc, rc, sp2, rp2, sp4, rp4, sd1, rd1, sd2, rd2, sd4, rd4,
@@ -61,6 +63,29 @@
             device_id=where, device_id_type=MESH,
         )
 
+    small = [
+        pltpu.make_async_copy(src, dst, sem_small.at[i])
+        for i, (src, dst) in enumerate(
+            ((len_in, len_ref), (wid_in, wid_ref), (pat_in, pat_ref), (bias_in, bias_ref))
+        )
+    ]
+    for copy in small:
+        copy.start()
+
+    def fetch(src, dst, sem):
+        copies = [
+            pltpu.make_async_copy(src.at[0, :, pl.ds(h * BLOCK, BLOCK)], dst(h), sem.at[h])
+            for h in range(heads)
+        ]
+        for copy in copies:
+            copy.start()
+        return copies
+
+    fetch_g = fetch(g_ref, lambda h: x0.at[h, 1], sem_g)
+    fetch_q = fetch(q_ref, lambda h: x0.at[h, 0], sem_q)
+    fetch_k = fetch(k_ref, lambda h: kh.at[h], sem_k)
+    fetch_v = fetch(v_ref, lambda h: vh.at[h], sem_v)
+
     barrier = pltpu.get_barrier_semaphore()
 
     @pl.loop(1, n_ctx)
@@ -75,6 +100,8 @@
             barrier, inc=1, device_id=(lax.rem(row + j, n_dp), me), device_id_type=MESH
         )
 
+    for copy in small:
+        copy.wait()
     slot = me // GROUP
     length = len_ref[0, slot]
     wide = (wid_ref[0, slot] >= 2).astype(F32)
@@ -82,13 +109,14 @@
     real = (places < length).astype(F32)
     real_bf = real.astype(BF16)
     for h in range(heads):
-        c = slice(h * BLOCK, (h + 1) * BLOCK)
-        x0[h, 0] = q_ref[0, :, c]
-        x0[h, 1] = g_ref[0, :, c] * real_bf
+        fetch_g[h].wait()
+        x0[h, 1] = x0[h, 1] * real_bf
     for b in range(blocks):
         for j in range(2):
             pt0[b * 2 + j : b * 2 + j + 1, :] = jnp.full((1, BLOCK), pat_ref[0, b, j].astype(F32))
 
+    for h in range(heads):
+        fetch_q[h].wait()
     pl.semaphore_wait(barrier, n_ctx - 1 + n_dp - 1)
 
     def copy_a(h):
@@ -141,9 +169,9 @@
             copy_c_odd(h).start()
 
     for h in range(heads):
-        c = slice(h * BLOCK, (h + 1) * BLOCK)
-        kh[h] = k_ref[0, :, c]
-        vh[h] = v_ref[0, :, c] * real_bf
+        fetch_k[h].wait()
+        fetch_v[h].wait()
+        vh[h] = vh[h] * real_bf
     ab[...] = jnp.zeros_like(ab)
 
     kpos = lax.broadcasted_iota(jnp.int32, (tokens, tokens), 0)
@@ -168,6 +196,18 @@
         av[h] = gv
         add_bias(h, 0, colsum(ds[:BLOCK, :BLOCK]) + colsum(ds[BLOCK:, BLOCK:]))
         add_bias(h, 1, colsum(ds[:BLOCK, BLOCK:]))
+
+        @pl.when(from2)
+        def _():
+            copy_a(h).wait_recv()
+
+            @pl.when(to2)
+            def _():
+                copy_b(h).start()
+
+            @pl.when(even)
+            def _():
+                copy_c_even(h).start()
 
     out_scale = scaling / SEQ
 
@@ -202,16 +242,6 @@
     def _(h):
         @pl.when(from2)
         def _():
-            copy_a(h).wait_recv()
-
-            @pl.when(to2)
-            def _():
-                copy_b(h).start()
-
-            @pl.when(even)
-            def _():
-                copy_c_even(h).start()
-
             far(h, x2, pt2, 2, 0, d2)
             copy_d(h, 2).start()
 
@@ -347,6 +377,30 @@
         copy_bd(j, row).wait_send()
 
 
+def copy_kernel(*refs):
+    *refs, sems = refs
+    half = len(refs) // 2
+    copies = [
+        pltpu.make_async_copy(refs[i], refs[half + i], sems.at[i]) for i in range(half)
+    ]
+    for copy in copies:
+        copy.start()
+    for copy in copies:
+        copy.wait()
+
+
+def copy_out(arrays):
+    any_ = pl.BlockSpec(memory_space=pl.ANY)
+    n = len(arrays)
+    return pl.pallas_call(
+        copy_kernel,
+        out_shape=tuple(jax.ShapeDtypeStruct(a.shape, a.dtype) for a in arrays),
+        in_specs=[any_] * n,
+        out_specs=(any_,) * n,
+        scratch_shapes=[pltpu.SemaphoreType.DMA((n,))],
+    )(*arrays)
+
+
 def on_device(
     queries, key_vectors, value_vectors, grad_output, pattern, lengths, widths, relative_bucket_bias,
     n_dp, n_ctx,
@@ -355,7 +409,7 @@
     heads = relative_bucket_bias.shape[0]
     dim = width // heads
     vm = pl.BlockSpec(memory_space=pltpu.VMEM)
-    sm = pl.BlockSpec(memory_space=pltpu.SMEM)
+    hbm = pl.BlockSpec(memory_space=pl.ANY)
     dma = pltpu.SemaphoreType.DMA
     x = pltpu.VMEM((heads, 2, tokens, dim), BF16)
     half = pltpu.VMEM((heads, tokens, dim), BF16)
@@ -363,12 +417,16 @@
     pat = pltpu.VMEM((8, BLOCK), F32)
     per_head = dma((heads,))
     rows = jax.ShapeDtypeStruct(queries.shape, BF16)
-    return pl.pallas_call(
+    small = (lengths, widths, pattern, relative_bucket_bias)
+    results = pl.pallas_call(
         functools.partial(kernel, n_dp, n_ctx, heads, tokens, dim ** (-0.5)),
         out_shape=(rows, rows, rows, jax.ShapeDtypeStruct(relative_bucket_bias.shape, F32)),
-        in_specs=[sm] * 4 + [vm] * 4,
+        in_specs=[hbm] * 8,
         out_specs=(vm,) * 4,
-        scratch_shapes=[half, half, x, x, x, x, pat, pat, pat]
+        scratch_shapes=[pltpu.SMEM(a.shape, a.dtype) for a in small]
+        + [dma((len(small),))]
+        + [per_head] * 4
+        + [half, half, x, x, x, x, pat, pat, pat]
         + [half] * 6
         + [acc] * 3
         + [
@@ -383,9 +441,10 @@
         + [per_head] * 6
         + [dma((n_ctx,)), dma((n_ctx,)), dma((n_dp,)), dma((n_dp,))],
         compiler_params=pltpu.CompilerParams(
-            collective_id=0, has_side_effects=True, vmem_limit_bytes=40 * 2**20
+            collective_id=0, has_side_effects=True, vmem_limit_bytes=VMEM_LIMIT
         ),
-    )(lengths, widths, pattern, relative_bucket_bias, queries, key_vectors, value_vectors, grad_output)
+    )(*small, queries, key_vectors, value_vectors, grad_output)
+    return copy_out(results)
 
 
 def solution(mesh):

time: 47 us -> 70.7 us (1.50)
  Pallas kernels: 37.9 us -> 68.5 us
  local copies, waits for them, and re-layouts: 6.49 us -> 0 us
    pallas_call x0 -> x1, Pallas kernels: none -> 25 us  [copy_out(): pl.pallas_call(copy_kernel, out_shape=tuple((jax.ShapeDtypeStruct(a.shape...]
    unnamed x16 -> x0, local copies, waits for them, and re-layouts: 6.49 us -> none
    pallas_call x1, Pallas kernels: 37.9 us -> 43.5 us  [on_device(): pl.pallas_call(functools.partial(kernel, n_dp, n_ctx, heads, tokens, dim...]
where the time goes in v2:
time: 70.7 us; the launch traced here: 70.5 us
  Pallas kernels  68.5 us (97%)
  between operations  1.93 us (3%)
    pallas_call x1, Pallas kernels, on_device(): pl.pallas_call(functools.partial(kernel, n_dp, n_ctx, heads, tokens, dim...  43.5 us
    pallas_call x1, Pallas kernels, copy_out(): pl.pallas_call(copy_kernel, out_shape=tuple((jax.ShapeDtypeStruct(a.shape...  25 us

profile of v2, /device:TPU:16, one launch (start us, length us, event | category | flops | bytes accessed | tf_op | source)
XLA Modules:
  0.0 70.5 jit_solution(15443118469272375708)
XLA Ops:
  1.9 43.5 %shard_map.111 = (bf16[1,256,512]{2,1,0:T(8,128)(2,1)}, bf16[1,256,512]{2,1,0:T(8,128)(2,1)}, bf16[1,256,512]{2,1,0:T(8,128)(2,1)}, f32[4,7]{1,0:T(4,128)}) custom-call(s32[1,1]{1,0:T(1,128)S(6)} %copy.12.len_in, s32[1,1]{1,0:T(1,128)S(6)} %copy.13.wid_in, s32[1,2,2]{2,1,0:T(2,128)} %pat_in.1, f32[4,7]{1,0:T(4,128)} %bias_in.1, bf16[1,256,512]{2,1,0:T(8,128)(2,1)} %q_ref.1, ...), custom_call_target="tpu_custom_call" | custom-call | tf_op jit(solution)/shard_map/pallas_call | solution.py:421
  45.4 25.0 %shard_map.112 = (bf16[1,256,512]{2,1,0:T(8,128)(2,1)}, bf16[1,256,512]{2,1,0:T(8,128)(2,1)}, bf16[1,256,512]{2,1,0:T(8,128)(2,1)}, f32[4,7]{1,0:T(4,128)}) custom-call(bf16[1,256,512]{2,1,0:T(8,128)(2,1)} %get-tuple-element.8.refs_0_, bf16[1,256,512]{2,1,0:T(8,128)(2,1)} %get-tuple-element.9.refs_1_, bf16[1,256,512]{2,1,0:T(8,128)(2,1)} %get-tuple-element.10.refs_2_, ...), custom_call_target="tpu_custom_call" | custom-call | tf_op jit(solution)/shard_map/pallas_call | solution.py:395

commit v3 on v2

--- a/solution.py
+++ b/solution.py
@@ -184,30 +184,6 @@
 
     def add_bias(h, bucket, value):
         ab[h, bucket : bucket + 1, :] += value
-
-    @pl.loop(0, heads)
-    def _(h):
-        bias = jnp.where(qb > kb, bias_ref[h, 1], bias_ref[h, 0])
-        gq, gk, gv, ds = tile(
-            x0[h, 0], x0[h, 1], kh[h], vh[h], bias, scaling, kpos <= qpos
-        )
-        aq[h] = gq
-        ak[h] = gk
-        av[h] = gv
-        add_bias(h, 0, colsum(ds[:BLOCK, :BLOCK]) + colsum(ds[BLOCK:, BLOCK:]))
-        add_bias(h, 1, colsum(ds[:BLOCK, BLOCK:]))
-
-        @pl.when(from2)
-        def _():
-            copy_a(h).wait_recv()
-
-            @pl.when(to2)
-            def _():
-                copy_b(h).start()
-
-            @pl.when(even)
-            def _():
-                copy_c_even(h).start()
 
     out_scale = scaling / SEQ
 
@@ -234,17 +210,7 @@
                 add_bias(h, u0, total * c0)
                 add_bias(h, u1, total * c1)
 
-    @pl.when(from2)
-    def _():
-        copy_p2().wait_recv()
-
-    @pl.loop(0, heads)
-    def _(h):
-        @pl.when(from2)
-        def _():
-            far(h, x2, pt2, 2, 0, d2)
-            copy_d(h, 2).start()
-
+    def near(h):
         @pl.when(from1)
         def _():
             copy_c_odd(h).wait_recv()
@@ -260,6 +226,39 @@
             add_bias(h, 1, colsum(ds[BLOCK:, :BLOCK]))
             add_bias(h, 2, colsum(ds[:BLOCK, :BLOCK]) + colsum(ds[BLOCK:, BLOCK:]))
 
+    @pl.when(from2)
+    def _():
+        copy_p2().wait_recv()
+
+    @pl.loop(0, heads)
+    def _(h):
+        bias = jnp.where(qb > kb, bias_ref[h, 1], bias_ref[h, 0])
+        gq, gk, gv, ds = tile(
+            x0[h, 0], x0[h, 1], kh[h], vh[h], bias, scaling, kpos <= qpos
+        )
+        aq[h] = gq
+        ak[h] = gk
+        av[h] = gv
+        add_bias(h, 0, colsum(ds[:BLOCK, :BLOCK]) + colsum(ds[BLOCK:, BLOCK:]))
+        add_bias(h, 1, colsum(ds[:BLOCK, BLOCK:]))
+
+        @pl.when(from2)
+        def _():
+            copy_a(h).wait_recv()
+
+            @pl.when(to2)
+            def _():
+                copy_b(h).start()
+
+            @pl.when(even)
+            def _():
+                copy_c_even(h).start()
+
+            far(h, x2, pt2, 2, 0, d2)
+            copy_d(h, 2).start()
+
+        near(h)
+
     @pl.when(from4)
     def _():
         copy_p4().wait_recv()
@@ -377,27 +376,30 @@
         copy_bd(j, row).wait_send()
 
 
-def copy_kernel(*refs):
-    *refs, sems = refs
-    half = len(refs) // 2
-    copies = [
-        pltpu.make_async_copy(refs[i], refs[half + i], sems.at[i]) for i in range(half)
-    ]
-    for copy in copies:
+def copy_kernel(n, *refs):
+    src, dst, held, sems = refs[:n], refs[n : 2 * n], refs[2 * n : 3 * n], refs[3 * n]
+    come = [pltpu.make_async_copy(src[i], held[i], sems.at[0, i]) for i in range(n)]
+    go = [pltpu.make_async_copy(held[i], dst[i], sems.at[1, i]) for i in range(n)]
+    for copy in come:
         copy.start()
-    for copy in copies:
+    for i in range(n):
+        come[i].wait()
+        go[i].start()
+    for copy in go:
         copy.wait()
 
 
 def copy_out(arrays):
-    any_ = pl.BlockSpec(memory_space=pl.ANY)
+    anywhere = pl.BlockSpec(memory_space=pl.ANY)
     n = len(arrays)
     return pl.pallas_call(
-        copy_kernel,
+        functools.partial(copy_kernel, n),
         out_shape=tuple(jax.ShapeDtypeStruct(a.shape, a.dtype) for a in arrays),
-        in_specs=[any_] * n,
-        out_specs=(any_,) * n,
-        scratch_shapes=[pltpu.SemaphoreType.DMA((n,))],
+        in_specs=[anywhere] * n,
+        out_specs=(anywhere,) * n,
+        scratch_shapes=[pltpu.VMEM(a.shape, a.dtype) for a in arrays]
+        + [pltpu.SemaphoreType.DMA((2, n))],
+        compiler_params=pltpu.CompilerParams(vmem_limit_bytes=VMEM_LIMIT),
     )(*arrays)
 
 

time: 70.7 us -> 42.9 us (0.61)
  Pallas kernels: 68.5 us -> 40.3 us
    pallas_call x1, Pallas kernels: 25 us -> 1.9 us  [copy_out(): pl.pallas_call(functools.partial(copy_kernel, n), out_shape=tuple((jax.Sh...]
    pallas_call x1, Pallas kernels: 43.5 us -> 38.4 us  [on_device(): pl.pallas_call(functools.partial(kernel, n_dp, n_ctx, heads, tokens, dim...]
where the time goes in v3:
time: 42.9 us; the launch traced here: 42.2 us
  Pallas kernels  40.3 us (94%)
  between operations  1.93 us (4%)
    pallas_call x1, Pallas kernels, on_device(): pl.pallas_call(functools.partial(kernel, n_dp, n_ctx, heads, tokens, dim...  38.4 us
    pallas_call x1, Pallas kernels, copy_out(): pl.pallas_call(functools.partial(copy_kernel, n), out_shape=tuple((jax.Sh...  1.9 us

profile of v3, /device:TPU:16, one launch (start us, length us, event | category | flops | bytes accessed | tf_op | source)
XLA Modules:
  0.0 42.2 jit_solution(13284115681598708913)
XLA Ops:
  1.9 38.4 %shard_map.111 = (bf16[1,256,512]{2,1,0:T(8,128)(2,1)}, bf16[1,256,512]{2,1,0:T(8,128)(2,1)}, bf16[1,256,512]{2,1,0:T(8,128)(2,1)}, f32[4,7]{1,0:T(4,128)}) custom-call(s32[1,1]{1,0:T(1,128)S(6)} %copy.12.len_in, s32[1,1]{1,0:T(1,128)S(6)} %copy.13.wid_in, s32[1,2,2]{2,1,0:T(2,128)} %pat_in.1, f32[4,7]{1,0:T(4,128)} %bias_in.1, bf16[1,256,512]{2,1,0:T(8,128)(2,1)} %q_ref.1, ...), custom_call_target="tpu_custom_call" | custom-call | tf_op jit(solution)/shard_map/pallas_call | solution.py:423
  40.3 1.9 %shard_map.112 = (bf16[1,256,512]{2,1,0:T(8,128)(2,1)}, bf16[1,256,512]{2,1,0:T(8,128)(2,1)}, bf16[1,256,512]{2,1,0:T(8,128)(2,1)}, f32[4,7]{1,0:T(4,128)}) custom-call(bf16[1,256,512]{2,1,0:T(8,128)(2,1)} %get-tuple-element.8.refs_0_, bf16[1,256,512]{2,1,0:T(8,128)(2,1)} %get-tuple-element.9.refs_1_, bf16[1,256,512]{2,1,0:T(8,128)(2,1)} %get-tuple-element.10.refs_2_, ...), custom_call_target="tpu_custom_call" | custom-call | tf_op jit(solution)/shard_map/pallas_call | solution.py:395
